TPU v7x, 32 devices: a whole 2x2x4 slice. The times are simulated.
32 devices in a mesh: groups: 2 (over x), fsdp: 16 (over z, y, core).
Axes of the slice: x: 2, y: 2, z: 4, core: 2. Of those that a mesh axis runs over, the one named last changes fastest.
Arguments:
- layer_input: bfloat16 [12288, 2048], P(('groups', 'fsdp')), parts along dimension 0, may hold values from -6 to 6
- output_gradient: bfloat16 [12288, 6656], P(('groups', 'fsdp')), parts along dimension 0, may hold values from -6 to 6
- frozen_weight: bfloat16 [2048, 6656], P('fsdp'), may hold values from -0.078125 to 0.078125
- adapter_down: bfloat16 [4096, 64], P(('groups', 'fsdp')), parts along dimension 0, may hold values from -0.125 to 0.125
- adapter_up_matrix: bfloat16 [128, 6656], P('groups', 'fsdp'), parts along dimension 0, may hold values from -0.078125 to 0.078125
Outputs:
- grad_input: bfloat16 [12288, 2048], P(('groups', 'fsdp')), parts along dimension 0
- grad_down: float32 [4096, 64], P(('groups', 'fsdp')), parts along dimension 0
- up_matrix_gradient: float32 [128, 6656], P('groups', 'fsdp'), parts along dimension 0
There are 2 independent parts, one for each index of `groups`. A program takes and returns all parts, laid end to end along the dimension named above; an argument that names none is the same for every part. Nothing has to cross between parts.
All inputs are finite; a program needn't handle non-finite values.
Results may differ from a plain program's by a relative error of at most 0.0034.
Values may be sent and summed in bfloat16 or wider, within the bound.
A program may use at most 128 MiB of HBM per device.

v0:
```python
import math

import jax
import jax.numpy as jnp
from jax import lax
from jax.sharding import PartitionSpec as P

adapter_scale = 2.0


def contract_rows(left, right):
    return lax.dot_general(
        left, right, (((1,), (1,)), ((), ())), preferred_element_type=jnp.float32
    )


def token_contraction(left, right):
    return lax.dot_general(
        left, right, (((0,), (0,)), ((), ())), preferred_element_type=jnp.float32
    )


def reduce_grads(
    layer_input, hidden_projection, incoming_gradient, output_gradient, objective_scale
):
    part_down = token_contraction(layer_input, incoming_gradient) * objective_scale
    local_up_part = (
        adapter_scale * token_contraction(hidden_projection, output_gradient) * objective_scale
    )
    return (
        lax.psum_scatter(part_down, "fsdp", scatter_dimension=0, tiled=True),
        lax.psum_scatter(local_up_part, "fsdp", scatter_dimension=1, tiled=True),
    )


def shards(layer_input, output_gradient, frozen_weight, adapter_down, adapter_up_matrix):
    down_all, gathered_up_matrix = (
        lax.all_gather(adapter_down, "fsdp", axis=0, tiled=True),
        lax.all_gather(adapter_up_matrix, "fsdp", axis=1, tiled=True),
    )
    total_tokens = layer_input.shape[0] * lax.axis_size("fsdp")
    objective_scale = 1.0 / math.sqrt(total_tokens)
    hidden_projection = jnp.dot(layer_input, down_all, preferred_element_type=jnp.float32).astype(
        jnp.bfloat16
    )
    incoming_gradient = (adapter_scale * contract_rows(output_gradient, gathered_up_matrix)).astype(
        jnp.bfloat16
    )
    low_rank = contract_rows(incoming_gradient, down_all)
    dense_part = contract_rows(
        output_gradient, lax.all_gather(frozen_weight, "fsdp", axis=0, tiled=True)
    )
    grad_input = (dense_part + low_rank).astype(jnp.bfloat16)
    grad_down, up_matrix_gradient = reduce_grads(
        layer_input, hidden_projection, incoming_gradient, output_gradient, objective_scale
    )
    return (grad_input, grad_down, up_matrix_gradient)


def solution(mesh):
    in_specs = (
        P(("groups", "fsdp"), None),
        P(("groups", "fsdp"), None),
        P("fsdp", None),
        P(("groups", "fsdp"), None),
        P("groups", "fsdp"),
    )
    out_specs = (P(("groups", "fsdp"), None), P(("groups", "fsdp"), None), P("groups", "fsdp"))
    return jax.shard_map(shards, mesh=mesh, in_specs=in_specs, out_specs=out_specs, check_vma=False)
```

profile of v0, /device:TPU:0, one launch (start us, length us, event | category | flops | bytes accessed | tf_op | source)
XLA Modules:
  0.0 308.4 jit_solution(5139025520584831663)
XLA Ops:
  7.2 0.0 copy-start
  7.2 0.0 reduce-scatter.7.cloned.1.call-start
  7.2 24.2 %all_gather.11 = bf16[2048,64]{0,1:T(8,128)(2,1)S(1)} all-gather(bf16[128,64]{0,1:T(8,128)(2,1)} %param.8), channel_id=1, replica_groups=mesh['groups'=2,'fsdp'=16] {'fsdp'}, dimensions={0}, use_global_device_ids=true | all-gather | bytes 278528 | tf_op jit(solution)/shard_map/all_gather | solution.py:38
  31.4 0.0 copy-done
  31.4 0.0 copy-start.1
  31.4 4.2 %convolution_multiply_fusion = f32[64,6656]{1,0:T(8,128)S(1)} fusion(bf16[384,6656]{1,0:T(8,128)(2,1)} %param.6, bf16[384,2048]{1,0:T(8,128)(2,1)S(1)} %copy-done, bf16[2048,64]{0,1:T(8,128)(2,1)S(1)} %all_gather.11), kind=kOutput, calls=%fused_computation | convolution fusion | flops 428269568 | bytes 8650752 | tf_op jit(solution)/shard_map/dot_general | solution.py:18
  35.6 0.0 copy-done.1
  35.6 2.5 copy.10
  38.1 0.0 copy-start.3
  38.1 0.0 reduce-scatter.7.cloned.1.call-update
  38.1 0.0 all-gather.3.cloned.1.call-start
  38.2 0.7 all-gather.3.cloned.1.call-update
  38.9 0.0 reduce-scatter.5.cloned.1.call-start
  38.9 0.0 copy-done.3
  39.0 20.5 %all-gather = bf16[16,416,64]{1,2,0:T(8,128)(2,1)S(1)} all-gather(bf16[1,416,64]{1,2,0:T(8,128)(2,1)S(1)} %bitcast.22), channel_id=1, replica_groups=mesh['groups'=2,'fsdp'=16] {'fsdp'}, dimensions={0}, use_global_device_ids=true | all-gather | bytes 905216 | tf_op jit(solution)/shard_map/all_gather | solution.py:39
  59.5 0.6 copy.9
  60.0 1.3 reshape.7
  61.3 4.1 %fusion.1 = bf16[384,64]{0,1:T(8,128)(2,1)S(1)} fusion(bf16[384,6656]{1,0:T(8,128)(2,1)} %param.6, bf16[6656,64]{0,1:T(8,128)(2,1)S(1)} %reshape.7), kind=kOutput, calls=%fused_computation.5 | convolution fusion | flops 327204864 | bytes 6012928 | tf_op jit(solution)/shard_map/dot_general | solution.py:12
  65.4 1.2 fusion
  66.7 0.0 reduce-scatter.5.cloned.1.call-update
  66.7 36.2 %reduce-scatter.7.cloned.1.call-done = f32[416,64]{1,0:T(8,128)} async-done(((f32[6656,64]{1,0:T(8,128)}), f32[416,64]{1,0:T(8,128)}) %reduce-scatter.7.cloned.1.call-update) | async-done | bytes 106512
  102.9 1.7 copy.11
  104.6 0.0 copy-start.2
  104.6 137.3 %all-gather.3.cloned.1.call-done = bf16[2048,6656]{1,0:T(8,128)(2,1)} async-done(((bf16[128,6656]{1,0:T(8,128)(2,1)}), bf16[2048,6656]{1,0:T(8,128)(2,1)}) %all-gather.3.cloned.1.call-update) | async-done | bytes 27262992 | tf_op jit(solution)/shard_map/all_gather | solution.py:51
  241.9 15.9 %fusion.2 = f32[384,2048]{1,0:T(8,128)S(1)} fusion(bf16[384,6656]{1,0:T(8,128)(2,1)} %param.6, bf16[2048,6656]{1,0:T(8,128)(2,1)} %all-gather.3.cloned.1.call-done), kind=kOutput, calls=%fused_computation.7 | convolution fusion | flops 10468982784 | bytes 35520512 | tf_op jit(solution)/shard_map/dot_general | solution.py:12
  257.8 0.0 copy-done.2
  257.8 1.7 add_convert_fusion
  259.5 42.3 %reduce-scatter.5.cloned.1.call-done = f32[128,64]{0,1:T(8,128)} async-done(((f32[2048,64]{0,1:T(8,128)}), f32[128,64]{0,1:T(8,128)}) %reduce-scatter.5.cloned.1.call-update) | async-done | bytes 32784 | tf_op jit(solution)/shard_map/reduce_scatter | solution.py:31
Async XLA Ops:
  7.2 24.2 %copy-start = (bf16[384,2048]{1,0:T(8,128)(2,1)S(1)}, bf16[384,2048]{1,0:T(8,128)(2,1)}, u32[]{:S(2)}) copy-start(bf16[384,2048]{1,0:T(8,128)(2,1)} %param.5) | copy-start | bytes 4718596
  7.2 95.7 %reduce-scatter.7.cloned.1.call-start = ((), (), s32[]{:S(2)}) async-start(), calls=%async_computation.4 | async-start | bytes 3620864
  31.4 4.2 %copy-start.1 = (bf16[2048,64]{0,1:T(8,128)(2,1)}, bf16[2048,64]{0,1:T(8,128)(2,1)S(1)}, u32[]{:S(2)}) copy-start(bf16[2048,64]{0,1:T(8,128)(2,1)S(1)} %all_gather.11) | copy-start | bytes 786436
  38.1 0.8 copy-start.3
  38.1 203.7 %all-gather.3.cloned.1.call-start = ((), (), s32[]{:S(2)}) async-start(), calls=%async_computation.2 | async-start | bytes 28966912 | tf_op jit(solution)/shard_map/all_gather | solution.py:51
  38.9 262.9 %reduce-scatter.5.cloned.1.call-start = ((), (), s32[]{:S(2)}) async-start(), calls=%async_computation.3 | async-start | bytes 557056 | tf_op jit(solution)/shard_map/reduce_scatter | solution.py:31
  104.6 153.2 %copy-start.2 = (bf16[2048,64]{0,1:T(8,128)(2,1)S(1)}, bf16[2048,64]{0,1:T(8,128)(2,1)}, u32[]{:S(2)}) copy-start(bf16[2048,64]{0,1:T(8,128)(2,1)} %copy-done.1) | copy-start | bytes 786436
Sparse Core Ops, SparseCore 0:
  38.3 64.5 reduce-scatter.6
  104.5 137.3 all-gather.2
  246.0 55.7 reduce-scatter.4
where the time goes:
time: 309 us; the launch traced here: 308 us
  waiting for transfers between devices  217 us (70%)
  blocking collectives  44.7 us (14%)
  matrix products  27.2 us (9%)
  between operations  13.8 us (4%)
  local copies, waits for them, and re-layouts  6.08 us (2%)
    all_gather x1, waiting for transfers between devices, shards(): lax.all_gather(frozen_weight, 'fsdp', axis=0, tiled=True)  137 us
    reduce_scatter x1, waiting for transfers between devices, reduce_grads(): lax.psum_scatter(part_down, 'fsdp', scatter_dimension=0, tiled=True)  42.3 us
    unnamed x4, waiting for transfers between devices  36.9 us
    all_gather x1, blocking collectives, shards(): lax.all_gather(adapter_down, 'fsdp', axis=0, tiled=True)  24.2 us
    dot_general x3, matrix products, contract_rows(): lax.dot_general(left, right, (((1,), (1,)), ((), ())), preferred_element_...  21.8 us
    all_gather x1, blocking collectives, shards(): lax.all_gather(adapter_up_matrix, 'fsdp', axis=1, tiled=True)  20.5 us
  transfers between devices with their start and end apart: 3, of which 3 were waited for; matrix products, arithmetic and copies ran while one was open for 9% of the time, Pallas kernels for 0%

commit v1 on v0

v1 whole, which is shorter than its diff:
```python
import functools
import math

import jax
import jax.numpy as jnp
from jax import lax
from jax.experimental import pallas as pl
from jax.experimental.pallas import tpu as pltpu
from jax.sharding import PartitionSpec as P

adapter_scale = 2.0
MESH = pl.DeviceIdType.MESH
HALVES = 2


def dot_nt(left, right):
    return lax.dot_general(
        left, right, (((1,), (1,)), ((), ())), preferred_element_type=jnp.float32
    )


def dot_tn(left, right):
    return lax.dot_general(
        left, right, (((0,), (0,)), ((), ())), preferred_element_type=jnp.float32
    )


def chip_at(position, chips, two_columns):
    if not two_columns:
        return position
    return jnp.where(
        position < chips // 2, 2 * position, 2 * (chips - 1 - position) + 1
    )


def place_of(chip, chips, two_columns):
    if not two_columns:
        return chip
    row, column = chip // 2, chip % 2
    return jnp.where(column == 0, row, chips - 1 - row)


def dense_kernel(
    chips, two_columns, rows, features, side, middle,
    grad_ref, weight_ref, upstream_ref, down_ref, out_ref,
    held, grad, local_sem, send_sem, recv_sem, own_send, own_recv,
):
    group, me = lax.axis_index("groups"), lax.axis_index("fsdp")
    core = lax.rem(me, 2)
    place = place_of(me // 2, chips, two_columns)
    role = lax.rem(group, 2)
    steps = chips - 1
    half = rows // HALVES

    def device(position):
        return chip_at(lax.rem(position + 2 * chips, chips), chips, two_columns) * 2 + core

    ahead, behind = (group, device(place + 1)), (group, device(place - 1))
    across = (group + 1 - 2 * role, me)
    sibling = (group, me + 1 - 2 * core)

    load_weight = pltpu.make_async_copy(
        weight_ref, held.at[pl.ds(pl.multiple_of(me * rows, rows), rows)], local_sem.at[0]
    )
    load_grad = pltpu.make_async_copy(grad_ref, grad, local_sem.at[1])
    load_weight.start()
    load_grad.start()

    barrier = pltpu.get_barrier_semaphore()
    for other in (ahead, behind, across, sibling):
        pl.semaphore_signal(barrier, inc=1, device_id=other, device_id_type=MESH)
    pl.semaphore_wait(barrier, 4)

    near = pl.multiple_of(role * (side + middle), 128)
    far = pl.multiple_of((1 - role) * (side + middle), 128)

    def block(owner, h, columns):
        return held.at[pl.ds(pl.multiple_of(owner * rows + h * half, half), half), columns]

    cut_near, cut_far, cut_mid = pl.ds(near, side), pl.ds(far, side), pl.ds(side, middle)

    def copy(kind, h, step, owner, columns, target):
        ref = block(owner, h, columns)
        return pltpu.make_async_remote_copy(
            src_ref=ref, dst_ref=ref,
            send_sem=send_sem.at[kind, h, step], recv_sem=recv_sem.at[kind, h, step],
            device_id=target, device_id_type=MESH,
        )

    def forward(h, step, owner):
        return copy(0, h, step, owner, cut_near, ahead)

    def backward(h, step, owner):
        return copy(1, h, step, owner, cut_mid, behind)

    def cross(h, step, owner):
        return copy(2, h, step, owner, cut_near, across)

    def cross_in(h, step, owner):
        return copy(2, h, step, owner, cut_far, across)

    def share(kind, h, step, owner, columns):
        return copy(3 + kind, h, step, owner, columns, sibling)

    def compute(distance):
        chip = chip_at(lax.rem(place - distance + 2 * chips, chips), chips, two_columns)
        both = pl.ds(pl.multiple_of(chip * 2 * rows, 2 * rows), 2 * rows)
        total = dot_nt(grad[...], held[both, :]) + dot_nt(upstream_ref[...], down_ref[both, :])
        out_ref[chip] = total.astype(out_ref.dtype)

    load_weight.wait()
    for h in range(HALVES):
        forward(h, 0, me).start()
        backward(h, 0, me).start()
    mine = held.at[pl.ds(pl.multiple_of(me * rows, rows), rows)]
    twin = me + 1 - 2 * core
    twins = held.at[pl.ds(pl.multiple_of(twin * rows, rows), rows)]
    own = pltpu.make_async_remote_copy(
        src_ref=mine, dst_ref=mine, send_sem=own_send, recv_sem=own_recv,
        device_id=sibling, device_id_type=MESH,
    )
    own_in = pltpu.make_async_remote_copy(
        src_ref=twins, dst_ref=twins, send_sem=own_send, recv_sem=own_recv,
        device_id=sibling, device_id_type=MESH,
    )
    own.start()
    load_grad.wait()
    own_in.wait_recv()
    compute(0)

    def pass_cross(step):
        from_behind = device(place - 1 - step)
        for h in range(HALVES):
            cross_in(h, step, from_behind).wait_recv()
            share(2, h, step, from_behind, cut_far).start()

    def wait_shared(distance):
        owner = device(place - distance) + 1 - 2 * core
        step, step_back = distance - 1, chips - distance - 1
        for h in range(HALVES):
            share(0, h, step, owner, cut_near).wait_recv()
            share(2, h, step, owner, cut_far).wait_recv()
            share(1, h, step_back, owner, cut_mid).wait_recv()

    def step_body(step, carry):
        from_behind, from_ahead = device(place - 1 - step), device(place + 1 + step)
        for h in range(HALVES):
            forward(h, step, from_behind).wait_recv()

            @pl.when(step + 1 < steps)
            def _():
                forward(h, step + 1, from_behind).start()

            cross(h, step, from_behind).start()
            share(0, h, step, from_behind, cut_near).start()
            backward(h, step, from_ahead).wait_recv()

            @pl.when(step + 1 < steps)
            def _():
                backward(h, step + 1, from_ahead).start()

            share(1, h, step, from_ahead, cut_mid).start()

        @pl.when(step >= 1)
        def _():
            pass_cross(step - 1)

        @pl.when(step >= chips // 2)
        def _():
            def both(k, carry):
                distance = jnp.where(k == 0, step, chips - 1 - step)
                wait_shared(distance)
                compute(distance)
                return carry

            lax.fori_loop(0, 2, both, 0)

        return carry

    lax.fori_loop(0, steps, step_body, 0)
    pass_cross(steps - 1)
    wait_shared(steps)
    compute(steps)

    def drain(step, carry):
        from_behind, from_ahead = device(place - 1 - step), device(place + 1 + step)
        for h in range(HALVES):
            forward(h, step, from_behind).wait_send()
            backward(h, step, from_ahead).wait_send()
            cross(h, step, from_behind).wait_send()
            share(0, h, step, from_behind, cut_near).wait_send()
            share(1, h, step, from_ahead, cut_mid).wait_send()
            share(2, h, step, from_behind, cut_far).wait_send()
        return carry

    lax.fori_loop(0, steps, drain, 0)
    own.wait_send()


def dense_part(groups, output_gradient, frozen_weight, upstream, down_all):
    tokens, features = output_gradient.shape
    rows = frozen_weight.shape[0]
    devices = down_all.shape[0] // rows
    chips = devices // 2
    side = features // 128 // 3 * 128
    middle = features - 2 * side
    steps = chips - 1
    vmem = pl.BlockSpec(memory_space=pltpu.VMEM)
    hbm = pl.BlockSpec(memory_space=pl.ANY)
    blocks = pl.pallas_call(
        functools.partial(dense_kernel, chips, groups == 2, rows, features, side, middle),
        out_shape=jax.ShapeDtypeStruct((chips, tokens, 2 * rows), jnp.bfloat16),
        in_specs=[hbm, hbm, vmem, vmem],
        out_specs=vmem,
        scratch_shapes=[
            pltpu.VMEM((devices * rows, features), jnp.bfloat16),
            pltpu.VMEM((tokens, features), jnp.bfloat16),
            pltpu.SemaphoreType.DMA((2,)),
            pltpu.SemaphoreType.DMA((6, HALVES, steps)),
            pltpu.SemaphoreType.DMA((6, HALVES, steps)),
            pltpu.SemaphoreType.DMA,
            pltpu.SemaphoreType.DMA,
        ],
        compiler_params=pltpu.CompilerParams(
            collective_id=0, has_side_effects=True, vmem_limit_bytes=52 * 1024 * 1024
        ),
        cost_estimate=pl.CostEstimate(
            flops=2 * tokens * features * devices * rows * 10,
            bytes_accessed=2 * features * devices * rows * 6, transcendentals=0,
        ),
    )(output_gradient, frozen_weight, upstream, down_all)
    return jnp.transpose(blocks, (1, 0, 2)).reshape(tokens, devices * rows)


def shards(groups, layer_input, output_gradient, frozen_weight, adapter_down, adapter_up_matrix):
    devices = lax.axis_size("fsdp")
    objective_scale = 1.0 / math.sqrt(layer_input.shape[0] * devices)
    rows, rank = adapter_down.shape
    packed = jnp.concatenate([adapter_down, adapter_up_matrix.T], axis=0)
    packed = lax.all_gather(packed, "fsdp", axis=0)
    down_all = packed[:, :rows].reshape(-1, rank)
    up_all = packed[:, rows:].reshape(-1, rank)
    latent = jnp.dot(layer_input, down_all, preferred_element_type=jnp.float32).astype(
        jnp.bfloat16
    )
    upstream = (
        adapter_scale * jnp.dot(output_gradient, up_all, preferred_element_type=jnp.float32)
    ).astype(jnp.bfloat16)
    part_down = dot_tn(layer_input, upstream) * objective_scale
    part_up = dot_tn(output_gradient, latent) * (adapter_scale * objective_scale)
    parts = jnp.concatenate(
        [part_down.reshape(devices, rows, rank), part_up.reshape(devices, -1, rank)], axis=1
    )
    parts, upstream = lax.optimization_barrier((parts, upstream))
    summed = lax.psum_scatter(parts, "fsdp", scatter_dimension=0, tiled=False)
    grad_input = dense_part(groups, output_gradient, frozen_weight, upstream, down_all)
    return (grad_input, summed[:rows], summed[rows:].T)


def solution(mesh):
    in_specs = (
        P(("groups", "fsdp"), None),
        P(("groups", "fsdp"), None),
        P("fsdp", None),
        P(("groups", "fsdp"), None),
        P("groups", "fsdp"),
    )
    out_specs = (P(("groups", "fsdp"), None), P(("groups", "fsdp"), None), P("groups", "fsdp"))
    return jax.shard_map(
        functools.partial(shards, mesh.shape["groups"]),
        mesh=mesh, in_specs=in_specs, out_specs=out_specs, check_vma=False,
    )
```

time: 309 us -> 208 us (0.67)
  waiting for transfers between devices: 217 us -> 43.5 us
  Pallas kernels: 0 us -> 120 us
  blocking collectives: 44.7 us -> 0 us
  matrix products: 27.2 us -> 9.91 us
  local copies, waits for them, and re-layouts: 6.08 us -> 17.2 us
  other arithmetic: 0 us -> 3.38 us
    pallas_call x0 -> x1, Pallas kernels: none -> 120 us  [dense_part(): pl.pallas_call(functools.partial(dense_kernel, chips, groups == 2, rows,...]
    all_gather x1, waiting for transfers between devices: 137 us -> 43.5 us  [shards(): packed = lax.all_gather(packed, 'fsdp', axis=0)]
    all_gather x2 -> x0, blocking collectives: 44.7 us -> none  [the longest x1 24.2 us: shards(): lax.all_gather(adapter_down, 'fsdp', axis=0, tiled=True)]
    reduce_scatter x1, waiting for transfers between devices: 42.3 us -> 0.01 us  [shards(): summed = lax.psum_scatter(parts, 'fsdp', scatter_dimension=0, tiled=False)]
    unnamed x4 -> x2, waiting for transfers between devices: 36.9 us -> 0.03 us
    dot_general x5 -> x3, matrix products: 27.2 us -> 9.91 us  [the longest x2 5.73 us: dot_tn(): lax.dot_general(left, right, (((0,), (0,)), ((), ())), preferred_element_...]
    reshape x0 -> x4, local copies, waits for them, and re-layouts: none -> 8.68 us  [the longest x2 6.47 us: shards(): part_up.reshape(devices, -1, rank)]
    unnamed x11 -> x3, local copies, waits for them, and re-layouts: 5.5 us -> 1.64 us
  transfers between devices with their start and end apart: 3 -> 2, of which waited for: 3 -> 1; matrix products, arithmetic and copies ran while one was open for 9% -> 2% of each run, Pallas kernels for 0% -> 58%
where the time goes in v1:
time: 208 us
  Pallas kernels  120 us (58%)
  waiting for transfers between devices  43.5 us (21%)
  local copies, waits for them, and re-layouts  17.2 us (8%)
  between operations  14.1 us (7%)
  matrix products  9.91 us (5%)
  other arithmetic  3.38 us (2%)
    pallas_call x1, Pallas kernels, dense_part(): pl.pallas_call(functools.partial(dense_kernel, chips, groups == 2, rows,...  120 us
    all_gather x1, waiting for transfers between devices, shards(): packed = lax.all_gather(packed, 'fsdp', axis=0)  43.5 us
    reshape x2, local copies, waits for them, and re-layouts, shards(): part_up.reshape(devices, -1, rank)  6.47 us
    dot_general x2, matrix products, dot_tn(): lax.dot_general(left, right, (((0,), (0,)), ((), ())), preferred_element_...  5.73 us
    dot_general x1, matrix products, shards(): jnp.dot(output_gradient, up_all, preferred_element_type=jnp.float32)  4.18 us
  transfers between devices with their start and end apart: 2, of which 1 were waited for; matrix products, arithmetic and copies ran while one was open for 2% of the time, Pallas kernels for 58%

profile of v1, /device:TPU:0, one launch (start us, length us, event | category | flops | bytes accessed | tf_op | source)
XLA Modules:
  0.0 208.0 jit_solution(17770533389050757541)
XLA Ops:
  7.2 0.0 copy-start
  7.2 0.0 all-gather.4.cloned.1.call-start
  7.2 1.6 maximum_bitcast_fusion
  8.8 0.0 all-gather.4.cloned.1.call-update
  8.8 0.0 reduce-scatter.2.cloned.1.call-start
  8.9 43.5 %all-gather.4.cloned.1.call-done = bf16[16,544,64]{1,2,0:T(8,128)(2,1)} async-done(((bf16[1,544,64]{1,2,0:T(8,128)(2,1)}), bf16[16,544,64]{1,2,0:T(8,128)(2,1)}) %all-gather.4.cloned.1.call-update) | async-done | bytes 1114128 | tf_op jit(solution)/shard_map/all_gather | solution.py:240
  52.4 0.0 slice-start
  52.4 1.2 slice-done
  53.6 0.6 copy.19
  54.2 0.0 slice-start.1
  54.2 2.2 %reshape.23 = bf16[6656,64]{0,1:T(8,128)(2,1)} reshape(bf16[16,416,64]{1,0,2:T(8,128)(2,1)S(1)} %copy.19) | data formatting | bytes 1703936 | tf_op jit(solution)/shard_map/reshape | solution.py:242
  56.4 0.0 slice-done.1
  56.4 0.3 copy.21
  56.7 4.2 %fusion.2 = bf16[64,384]{0,1:T(8,128)(2,1)S(1)} fusion(bf16[6656,64]{0,1:T(8,128)(2,1)} %reshape.23, bf16[384,6656]{1,0:T(8,128)(2,1)} %grad_ref.1), kind=kOutput, calls=%fused_computation.6 | convolution fusion | flops 327204864 | bytes 6012928 | tf_op jit(solution)/shard_map/dot_general | solution.py:247
  60.9 0.0 copy-done
  60.9 0.4 fusion.1
  61.4 5.3 %fusion = f32[6656,64]{0,1:T(8,128)} fusion(bf16[384,6656]{1,0:T(8,128)(2,1)} %grad_ref.1, bf16[2048,64]{1,0:T(8,128)(2,1)S(1)} %bitcast.32, bf16[384,2048]{1,0:T(8,128)(2,1)S(1)} %copy-done), kind=kOutput, calls=%fused_computation.1 | convolution fusion | flops 428269568 | bytes 8650752 | tf_op jit(solution)/shard_map/dot_general | solution.py:23
  66.7 3.7 %reshape.26 = f32[16,416,64]{1,0,2:T(8,128)} reshape(f32[6656,64]{0,1:T(8,128)} %fusion) | data formatting | bytes 3407872 | tf_op jit(solution)/shard_map/reshape | solution.py:252
  70.3 2.8 %copy.23 = f32[16,416,64]{1,2,0:T(8,128)S(1)} copy(f32[16,416,64]{1,0,2:T(8,128)} %reshape.26) | data formatting | bytes 3407872 | tf_op jit(solution)/shard_map/reshape | solution.py:252
  73.1 1.8 pad_maximum_fusion
  74.9 0.0 reduce-scatter.2.cloned.1.call-update
  74.9 119.7 %shard_map.76 = bf16[8,384,256]{2,1,0:T(8,128)(2,1)} custom-call(bf16[384,6656]{1,0:T(8,128)(2,1)} %grad_ref.1, bf16[128,6656]{1,0:T(8,128)(2,1)} %weight_ref.1, bf16[384,64]{1,0:T(8,128)(2,1)S(1)} %bitcast.34, bf16[2048,64]{1,0:T(8,128)(2,1)S(1)} %bitcast.33), custom_call_target="tpu_custom_call" | custom-call | flops 104689827840 | bytes 163577856 | tf_op jit(solution)/shard_map/pallas_call | solution.py:210
  194.7 1.9 copy.24
  196.6 1.6 copy.25
  198.2 0.0 reduce-scatter.2.cloned.1.call-done
  198.2 1.4 slice_bitcast_fusion.1
  199.6 1.6 slice_bitcast_fusion
  (1 shorter events, 0.0 us)
Async XLA Ops:
  7.2 53.7 %copy-start = (bf16[384,2048]{1,0:T(8,128)(2,1)S(1)}, bf16[384,2048]{1,0:T(8,128)(2,1)}, u32[]{:S(2)}) copy-start(bf16[384,2048]{1,0:T(8,128)(2,1)} %param.5) | copy-start | bytes 4718596
  7.2 45.2 %all-gather.4.cloned.1.call-start = ((), (), s32[]{:S(2)}) async-start(), calls=%async_computation.2 | async-start | bytes 1392640 | tf_op jit(solution)/shard_map/all_gather | solution.py:240
  8.8 189.4 %reduce-scatter.2.cloned.1.call-start = ((), (), s32[]{:S(2)}) async-start(), calls=%async_computation.1 | async-start | bytes 2785280 | tf_op jit(solution)/shard_map/reduce_scatter | solution.py:255
  52.4 1.2 slice-start
  54.2 2.2 %slice-start.1 = ((bf16[16,544,64]{1,2,0:T(8,128)(2,1)}), bf16[16,128,64]{1,2,0:T(8,128)(2,1)S(1)}, s32[]{:S(2)}) async-start(bf16[16,544,64]{1,2,0:T(8,128)(2,1)} %all-gather.4.cloned.1.call-done), calls=%async_computation.4 | async-start | bytes 524288 | tf_op jit(solution)/shard_map/slice | solution.py:241
Sparse Core Ops, SparseCore 0:
  10.9 41.4 all-gather.3
  75.1 76.4 reduce-scatter.1

commit v2 on v1

--- a/solution.py
+++ b/solution.py
@@ -106,7 +106,13 @@
         chip = chip_at(lax.rem(place - distance + 2 * chips, chips), chips, two_columns)
         both = pl.ds(pl.multiple_of(chip * 2 * rows, 2 * rows), 2 * rows)
         total = dot_nt(grad[...], held[both, :]) + dot_nt(upstream_ref[...], down_ref[both, :])
-        out_ref[chip] = total.astype(out_ref.dtype)
+        if len(out_ref.shape) == 2:
+            width = 2 * rows
+            out_ref[:, pl.ds(pl.multiple_of(chip * width, width), width)] = total.astype(
+                out_ref.dtype
+            )
+        else:
+            out_ref[chip] = total.astype(out_ref.dtype)
 
     load_weight.wait()
     for h in range(HALVES):
@@ -207,9 +213,11 @@
     steps = chips - 1
     vmem = pl.BlockSpec(memory_space=pltpu.VMEM)
     hbm = pl.BlockSpec(memory_space=pl.ANY)
+    lanes = 2 * rows % 128 == 0
+    shape = (tokens, devices * rows) if lanes else (chips, tokens, 2 * rows)
     blocks = pl.pallas_call(
         functools.partial(dense_kernel, chips, groups == 2, rows, features, side, middle),
-        out_shape=jax.ShapeDtypeStruct((chips, tokens, 2 * rows), jnp.bfloat16),
+        out_shape=jax.ShapeDtypeStruct(shape, jnp.bfloat16),
         in_specs=[hbm, hbm, vmem, vmem],
         out_specs=vmem,
         scratch_shapes=[
@@ -229,17 +237,124 @@
             bytes_accessed=2 * features * devices * rows * 6, transcendentals=0,
         ),
     )(output_gradient, frozen_weight, upstream, down_all)
+    if lanes:
+        return blocks
     return jnp.transpose(blocks, (1, 0, 2)).reshape(tokens, devices * rows)
+
+
+def gather_kernel(chips, two_columns, mine_ref, out_ref, send_sem, recv_sem, own_sem, local_sem):
+    group, me = lax.axis_index("groups"), lax.axis_index("fsdp")
+    core = lax.rem(me, 2)
+    place = place_of(me // 2, chips, two_columns)
+    forward_steps, backward_steps = chips // 2, chips - 1 - chips // 2
+
+    def device(position):
+        return chip_at(lax.rem(position + 2 * chips, chips), chips, two_columns) * 2 + core
+
+    ahead, behind = (group, device(place + 1)), (group, device(place - 1))
+    twin = me + 1 - 2 * core
+    sibling = (group, twin)
+
+    keep = pltpu.make_async_copy(mine_ref, out_ref.at[me], local_sem)
+    keep.start()
+    barrier = pltpu.get_barrier_semaphore()
+    for other in (ahead, behind, sibling):
+        pl.semaphore_signal(barrier, inc=1, device_id=other, device_id_type=MESH)
+    pl.semaphore_wait(barrier, 3)
+    keep.wait()
+
+    def copy(kind, step, owner, target):
+        return pltpu.make_async_remote_copy(
+            src_ref=out_ref.at[owner], dst_ref=out_ref.at[owner],
+            send_sem=send_sem.at[kind, step], recv_sem=recv_sem.at[kind, step],
+            device_id=target, device_id_type=MESH,
+        )
+
+    def own(owner):
+        return pltpu.make_async_remote_copy(
+            src_ref=out_ref.at[owner], dst_ref=out_ref.at[owner],
+            send_sem=own_sem.at[0], recv_sem=own_sem.at[1],
+            device_id=sibling, device_id_type=MESH,
+        )
+
+    copy(0, 0, me, ahead).start()
+    copy(1, 0, me, behind).start()
+    own(me).start()
+
+    def step_body(step, carry):
+        from_behind, from_ahead = device(place - 1 - step), device(place + 1 + step)
+        copy(0, step, from_behind, ahead).wait_recv()
+
+        @pl.when(step + 1 < forward_steps)
+        def _():
+            copy(0, step + 1, from_behind, ahead).start()
+
+        copy(2, step, from_behind, sibling).start()
+
+        @pl.when(step < backward_steps)
+        def _():
+            copy(1, step, from_ahead, behind).wait_recv()
+
+            @pl.when(step + 1 < backward_steps)
+            def _():
+                copy(1, step + 1, from_ahead, behind).start()
+
+            copy(3, step, from_ahead, sibling).start()
+
+        return carry
+
+    lax.fori_loop(0, forward_steps, step_body, 0)
+
+    def drain(step, carry):
+        from_behind, from_ahead = device(place - 1 - step), device(place + 1 + step)
+        swap = 1 - 2 * core
+        copy(0, step, from_behind, ahead).wait_send()
+        copy(2, step, from_behind, sibling).wait_send()
+        copy(2, step, from_behind + swap, sibling).wait_recv()
+
+        @pl.when(step < backward_steps)
+        def _():
+            copy(1, step, from_ahead, behind).wait_send()
+            copy(3, step, from_ahead, sibling).wait_send()
+            copy(3, step, from_ahead + swap, sibling).wait_recv()
+
+        return carry
+
+    lax.fori_loop(0, forward_steps, drain, 0)
+    own(me).wait_send()
+    own(twin).wait_recv()
+
+
+def gather_small(groups, devices, packed):
+    chips = devices // 2
+    vmem = pl.BlockSpec(memory_space=pltpu.VMEM)
+    return pl.pallas_call(
+        functools.partial(gather_kernel, chips, groups == 2),
+        out_shape=jax.ShapeDtypeStruct((devices, *packed.shape), packed.dtype),
+        in_specs=[vmem],
+        out_specs=vmem,
+        scratch_shapes=[
+            pltpu.SemaphoreType.DMA((4, chips // 2)),
+            pltpu.SemaphoreType.DMA((4, chips // 2)),
+            pltpu.SemaphoreType.DMA((2,)),
+            pltpu.SemaphoreType.DMA,
+        ],
+        compiler_params=pltpu.CompilerParams(
+            collective_id=1, has_side_effects=True, vmem_limit_bytes=16 * 1024 * 1024
+        ),
+    )(packed)
 
 
 def shards(groups, layer_input, output_gradient, frozen_weight, adapter_down, adapter_up_matrix):
     devices = lax.axis_size("fsdp")
     objective_scale = 1.0 / math.sqrt(layer_input.shape[0] * devices)
     rows, rank = adapter_down.shape
-    packed = jnp.concatenate([adapter_down, adapter_up_matrix.T], axis=0)
-    packed = lax.all_gather(packed, "fsdp", axis=0)
-    down_all = packed[:, :rows].reshape(-1, rank)
-    up_all = packed[:, rows:].reshape(-1, rank)
+    width = adapter_up_matrix.shape[1]
+    packed = jnp.concatenate([adapter_down.T, adapter_up_matrix], axis=1)
+    packed = jnp.pad(packed, ((0, 0), (0, -(rows + width) % 128)))
+    packed = gather_small(groups, devices, packed)
+    down_all = jnp.transpose(packed[:, :, :rows], (0, 2, 1)).reshape(-1, rank)
+    up_all = jnp.transpose(packed[:, :, rows : rows + width], (0, 2, 1)).reshape(-1, rank)
     latent = jnp.dot(layer_input, down_all, preferred_element_type=jnp.float32).astype(
         jnp.bfloat16
     )

time: 208 us -> 183 us (0.88)
  waiting for transfers between devices: 43.5 us -> 0.04 us
  Pallas kernels: 120 us -> 141 us
    all_gather x1 -> x0, waiting for transfers between devices: 43.5 us -> none  [shards(): packed = lax.all_gather(packed, 'fsdp', axis=0)]
    pallas_call x0 -> x1, Pallas kernels: none -> 20.4 us  [gather_small(): pl.pallas_call(functools.partial(gather_kernel, chips, groups == 2), out_...]
    slice x6 -> x0, local copies, waits for them, and re-layouts: 2.09 us -> none  [the longest x3 1.8 us: shards(): up_all = packed[:, rows:].reshape(-1, rank)]
  transfers between devices with their start and end apart: 2 -> 1, of which waited for: 1 -> 0; matrix products, arithmetic and copies ran while one was open for 2% -> 0% of each run, Pallas kernels for 58% -> 66%
where the time goes in v2:
time: 183 us
  Pallas kernels  141 us (77%)
  local copies, waits for them, and re-layouts  15.4 us (8%)
  between operations  14.1 us (8%)
  matrix products  9.91 us (5%)
  other arithmetic  2.74 us (1%)
    pallas_call x1, Pallas kernels, dense_part(): pl.pallas_call(functools.partial(dense_kernel, chips, groups == 2, rows,...  120 us
    pallas_call x1, Pallas kernels, gather_small(): pl.pallas_call(functools.partial(gather_kernel, chips, groups == 2), out_...  20.4 us
    reshape x2, local copies, waits for them, and re-layouts, shards(): part_up.reshape(devices, -1, rank)  6.5 us
    dot_general x2, matrix products, dot_tn(): lax.dot_general(left, right, (((0,), (0,)), ((), ())), preferred_element_...  5.73 us
    dot_general x1, matrix products, shards(): jnp.dot(output_gradient, up_all, preferred_element_type=jnp.float32)  4.18 us
  transfers between devices with their start and end apart: 1, of which 0 were waited for; matrix products, arithmetic and copies ran while one was open for 0% of the time, Pallas kernels for 66%

profile of v2, /device:TPU:0, one launch (start us, length us, event | category | flops | bytes accessed | tf_op | source)
XLA Modules:
  0.0 183.0 jit_solution(3285446506770340477)
XLA Ops:
  7.2 0.0 copy-start
  7.2 0.0 reduce-scatter.2.cloned.1.call-start
  7.2 1.0 fusion.5.mine_ref
  8.2 20.4 %shard_map.76 = bf16[16,64,640]{2,1,0:T(8,128)(2,1)S(1)} custom-call(bf16[64,640]{1,0:T(8,128)(2,1)S(1)} %fusion.5.mine_ref), custom_call_target="tpu_custom_call" | custom-call | tf_op jit(solution)/shard_map/pallas_call | solution.py:331
  28.6 0.1 slice_bitcast_fusion
  28.7 0.6 copy.12
  29.3 2.2 %reshape.20 = bf16[6656,64]{0,1:T(8,128)(2,1)} reshape(bf16[16,416,64]{1,0,2:T(8,128)(2,1)S(1)} %copy.12) | data formatting | bytes 1703936 | tf_op jit(solution)/shard_map/reshape | solution.py:357
  31.5 0.3 copy.14
  31.7 4.2 %fusion.2 = bf16[64,384]{0,1:T(8,128)(2,1)S(1)} fusion(bf16[6656,64]{0,1:T(8,128)(2,1)} %reshape.20, bf16[384,6656]{1,0:T(8,128)(2,1)} %grad_ref.1), kind=kOutput, calls=%fused_computation.6 | convolution fusion | flops 327204864 | bytes 6012928 | tf_op jit(solution)/shard_map/dot_general | solution.py:362
  35.9 0.0 copy-done
  35.9 0.4 fusion.1
  36.4 5.3 %fusion = f32[6656,64]{0,1:T(8,128)} fusion(bf16[384,6656]{1,0:T(8,128)(2,1)} %grad_ref.1, bf16[2048,64]{1,0:T(8,128)(2,1)S(1)} %bitcast.32, bf16[384,2048]{1,0:T(8,128)(2,1)S(1)} %copy-done), kind=kOutput, calls=%fused_computation.1 | convolution fusion | flops 428269568 | bytes 8650752 | tf_op jit(solution)/shard_map/dot_general | solution.py:23
  41.7 3.7 %reshape.23 = f32[16,416,64]{1,0,2:T(8,128)} reshape(f32[6656,64]{0,1:T(8,128)} %fusion) | data formatting | bytes 3407872 | tf_op jit(solution)/shard_map/reshape | solution.py:367
  45.4 2.8 %copy.16 = f32[16,416,64]{1,2,0:T(8,128)S(1)} copy(f32[16,416,64]{1,0,2:T(8,128)} %reshape.23) | data formatting | bytes 3407872 | tf_op jit(solution)/shard_map/reshape | solution.py:367
  48.2 1.8 pad_maximum_fusion
  50.0 0.0 reduce-scatter.2.cloned.1.call-update
  50.0 120.4 %shard_map.77 = bf16[384,2048]{1,0:T(8,128)(2,1)} custom-call(bf16[384,6656]{1,0:T(8,128)(2,1)} %grad_ref.1, bf16[128,6656]{1,0:T(8,128)(2,1)} %weight_ref.1, bf16[384,64]{1,0:T(8,128)(2,1)S(1)} %bitcast.34, bf16[2048,64]{1,0:T(8,128)(2,1)S(1)} %bitcast.33), custom_call_target="tpu_custom_call" | custom-call | flops 104689827840 | bytes 163577856 | tf_op jit(solution)/shard_map/pallas_call | solution.py:218
  170.5 0.0 reduce-scatter.2.cloned.1.call-done
  170.5 1.4 slice_bitcast_fusion.3
  171.9 1.6 slice_bitcast_fusion.2
  173.4 2.7 %copy.22 = bf16[384,2048]{1,0:T(8,128)(2,1)} copy(bf16[384,2048]{1,0:T(8,128)(2,1)} %shard_map.77) | data formatting | bytes 3145728
  (2 shorter events, 0.1 us)
Async XLA Ops:
  7.2 28.8 %copy-start = (bf16[384,2048]{1,0:T(8,128)(2,1)S(1)}, bf16[384,2048]{1,0:T(8,128)(2,1)}, u32[]{:S(2)}) copy-start(bf16[384,2048]{1,0:T(8,128)(2,1)} %param.5) | copy-start | bytes 4718596
  7.2 163.3 %reduce-scatter.2.cloned.1.call-start = ((), (), s32[]{:S(2)}) async-start(), calls=%async_computation.1 | async-start | bytes 2785280 | tf_op jit(solution)/shard_map/reduce_scatter | solution.py:370
Sparse Core Ops, SparseCore 0:
  50.2 75.8 reduce-scatter.1

commit v3 on v2

--- a/solution.py
+++ b/solution.py
@@ -11,6 +11,7 @@
 adapter_scale = 2.0
 MESH = pl.DeviceIdType.MESH
 HALVES = 2
+EARLY = 2
 
 
 def dot_nt(left, right):
@@ -42,7 +43,8 @@
 
 def dense_kernel(
     chips, two_columns, rows, features, side, middle,
-    grad_ref, weight_ref, upstream_ref, down_ref, out_ref,
+    grad_ref, weight_ref, upstream_ref, down_ref,
+    ahead_one, ahead_two, behind_one, behind_two, across_one, out_ref,
     held, grad, local_sem, send_sem, recv_sem, own_send, own_recv,
 ):
     group, me = lax.axis_index("groups"), lax.axis_index("fsdp")
@@ -65,6 +67,19 @@
     load_grad = pltpu.make_async_copy(grad_ref, grad, local_sem.at[1])
     load_weight.start()
     load_grad.start()
+    first, second = pl.ds(side, middle), pl.ds(pl.multiple_of(role * (side + middle), 128), side)
+    other = pl.ds(pl.multiple_of((1 - role) * (side + middle), 128), side)
+    early = []
+    for k, (ref, distance, columns) in enumerate((
+        (ahead_one, -1, second), (ahead_two, -2, second), (behind_one, 1, first),
+        (behind_two, 2, first), (across_one, -1, other),
+    )):
+        owner = device(place + distance)
+        early.append(pltpu.make_async_copy(
+            ref, held.at[pl.ds(pl.multiple_of(owner * rows, rows), rows), columns],
+            local_sem.at[2 + k],
+        ))
+        early[-1].start()
 
     barrier = pltpu.get_barrier_semaphore()
     for other in (ahead, behind, across, sibling):
@@ -115,9 +130,12 @@
             out_ref[chip] = total.astype(out_ref.dtype)
 
     load_weight.wait()
+    for load in early:
+        load.wait()
     for h in range(HALVES):
-        forward(h, 0, me).start()
-        backward(h, 0, me).start()
+        forward(h, EARLY, device(place - EARLY)).start()
+        backward(h, EARLY, device(place + EARLY)).start()
+        cross(h, EARLY - 1, device(place - EARLY)).start()
     mine = held.at[pl.ds(pl.multiple_of(me * rows, rows), rows)]
     twin = me + 1 - 2 * core
     twins = held.at[pl.ds(pl.multiple_of(twin * rows, rows), rows)]
@@ -139,6 +157,12 @@
         for h in range(HALVES):
             cross_in(h, step, from_behind).wait_recv()
             share(2, h, step, from_behind, cut_far).start()
+
+    for h in range(HALVES):
+        for step in range(EARLY):
+            share(0, h, step, device(place - 1 - step), cut_near).start()
+            share(1, h, step, device(place + 1 + step), cut_mid).start()
+        share(2, h, 0, device(place - 1), cut_far).start()
 
     def wait_shared(distance):
         owner = device(place - distance) + 1 - 2 * core
@@ -167,9 +191,7 @@
 
             share(1, h, step, from_ahead, cut_mid).start()
 
-        @pl.when(step >= 1)
-        def _():
-            pass_cross(step - 1)
+        pass_cross(step - 1)
 
         @pl.when(step >= chips // 2)
         def _():
@@ -183,7 +205,7 @@
 
         return carry
 
-    lax.fori_loop(0, steps, step_body, 0)
+    lax.fori_loop(EARLY, steps, step_body, 0)
     pass_cross(steps - 1)
     wait_shared(steps)
     compute(steps)
@@ -191,19 +213,49 @@
     def drain(step, carry):
         from_behind, from_ahead = device(place - 1 - step), device(place + 1 + step)
         for h in range(HALVES):
-            forward(h, step, from_behind).wait_send()
-            backward(h, step, from_ahead).wait_send()
-            cross(h, step, from_behind).wait_send()
             share(0, h, step, from_behind, cut_near).wait_send()
             share(1, h, step, from_ahead, cut_mid).wait_send()
             share(2, h, step, from_behind, cut_far).wait_send()
+
+            @pl.when(step >= EARLY)
+            def _():
+                forward(h, step, from_behind).wait_send()
+                backward(h, step, from_ahead).wait_send()
+
+            @pl.when(step >= EARLY - 1)
+            def _():
+                cross(h, step, from_behind).wait_send()
         return carry
 
     lax.fori_loop(0, steps, drain, 0)
     own.wait_send()
 
 
-def dense_part(groups, output_gradient, frozen_weight, upstream, down_all):
+def early_hops(groups, devices, frozen_weight):
+    chips = devices // 2
+    features = frozen_weight.shape[1]
+    side = features // 128 // 3 * 128
+    middle = features - 2 * side
+    ring = list(range(chips))
+    if groups == 2:
+        ring = list(range(0, chips, 2)) + list(range(chips - 1, 0, -2))
+    onward = [
+        (ring[k] * 2 + core, ring[(k + 1) % chips] * 2 + core)
+        for k in range(chips) for core in range(2)
+    ]
+    back = [(target, source) for source, target in onward]
+    role = lax.rem(lax.axis_index("groups"), 2)
+    near = jnp.where(role == 0, frozen_weight[:, :side], frozen_weight[:, side + middle :])
+    mid = frozen_weight[:, side : side + middle]
+    ahead_one = lax.ppermute(near, "fsdp", onward)
+    behind_one = lax.ppermute(mid, "fsdp", back)
+    across_one = lax.ppermute(ahead_one, "groups", [(g, g ^ 1) for g in range(groups)])
+    ahead_two = lax.ppermute(ahead_one, "fsdp", onward)
+    behind_two = lax.ppermute(behind_one, "fsdp", back)
+    return ahead_one, ahead_two, behind_one, behind_two, across_one
+
+
+def dense_part(groups, output_gradient, frozen_weight, upstream, down_all, early):
     tokens, features = output_gradient.shape
     rows = frozen_weight.shape[0]
     devices = down_all.shape[0] // rows
@@ -218,12 +270,12 @@
     blocks = pl.pallas_call(
         functools.partial(dense_kernel, chips, groups == 2, rows, features, side, middle),
         out_shape=jax.ShapeDtypeStruct(shape, jnp.bfloat16),
-        in_specs=[hbm, hbm, vmem, vmem],
+        in_specs=[hbm, hbm, vmem, vmem] + [hbm] * 5,
         out_specs=vmem,
         scratch_shapes=[
             pltpu.VMEM((devices * rows, features), jnp.bfloat16),
             pltpu.VMEM((tokens, features), jnp.bfloat16),
-            pltpu.SemaphoreType.DMA((2,)),
+            pltpu.SemaphoreType.DMA((7,)),
             pltpu.SemaphoreType.DMA((6, HALVES, steps)),
             pltpu.SemaphoreType.DMA((6, HALVES, steps)),
             pltpu.SemaphoreType.DMA,
@@ -236,7 +288,7 @@
             flops=2 * tokens * features * devices * rows * 10,
             bytes_accessed=2 * features * devices * rows * 6, transcendentals=0,
         ),
-    )(output_gradient, frozen_weight, upstream, down_all)
+    )(output_gradient, frozen_weight, upstream, down_all, *early)
     if lanes:
         return blocks
     return jnp.transpose(blocks, (1, 0, 2)).reshape(tokens, devices * rows)
@@ -342,6 +394,9 @@
         compiler_params=pltpu.CompilerParams(
             collective_id=1, has_side_effects=True, vmem_limit_bytes=16 * 1024 * 1024
         ),
+        cost_estimate=pl.CostEstimate(
+            flops=0, bytes_accessed=40 * 1024 * 1024, transcendentals=0
+        ),
     )(packed)
 
 
@@ -352,6 +407,7 @@
     width = adapter_up_matrix.shape[1]
     packed = jnp.concatenate([adapter_down.T, adapter_up_matrix], axis=1)
     packed = jnp.pad(packed, ((0, 0), (0, -(rows + width) % 128)))
+    early = early_hops(groups, devices, frozen_weight)
     packed = gather_small(groups, devices, packed)
     down_all = jnp.transpose(packed[:, :, :rows], (0, 2, 1)).reshape(-1, rank)
     up_all = jnp.transpose(packed[:, :, rows : rows + width], (0, 2, 1)).reshape(-1, rank)
@@ -368,7 +424,9 @@
     )
     parts, upstream = lax.optimization_barrier((parts, upstream))
     summed = lax.psum_scatter(parts, "fsdp", scatter_dimension=0, tiled=False)
-    grad_input = dense_part(groups, output_gradient, frozen_weight, upstream, down_all)
+    grad_input = dense_part(
+        groups, output_gradient, frozen_weight, upstream, down_all, early
+    )
     return (grad_input, summed[:rows], summed[rows:].T)
 
 

time: 183 us -> 178 us (0.973)
  Pallas kernels: 141 us -> 120 us
  starting transfers between devices: 0.04 us -> 6.97 us
  local copies, waits for them, and re-layouts: 15.4 us -> 21.4 us
  waiting for transfers between devices: 0.04 us -> 2.44 us
    pallas_call x1, Pallas kernels: 120 us -> 94 us  [dense_part(): pl.pallas_call(functools.partial(dense_kernel, chips, groups == 2, rows,...]
    ppermute x0 -> x5, starting transfers between devices: none -> 6.93 us  [the longest x1 3.08 us: early_hops(): ahead_one = lax.ppermute(near, 'fsdp', onward)]
    pallas_call x1, Pallas kernels: 20.4 us -> 26 us  [gather_small(): pl.pallas_call(functools.partial(gather_kernel, chips, groups == 2), out_...]
    transpose x2, local copies, waits for them, and re-layouts: 0.66 us -> 3.83 us  [shards(): jnp.transpose(packed[:, :, rows:rows + width], (0, 2, 1)).reshape(-1, rank)]
    ppermute x0 -> x5, waiting for transfers between devices: none -> 2.41 us  [the longest x1 2.13 us: early_hops(): behind_two = lax.ppermute(behind_one, 'fsdp', back)]
    slice x0 -> x1, local copies, waits for them, and re-layouts: none -> 1.95 us  [early_hops(): mid = frozen_weight[:, side:side + middle]]
  transfers between devices with their start and end apart: 1 -> 6, of which waited for: 0 -> 2; matrix products, arithmetic and copies ran while one was open for 0% -> 15% of each run, Pallas kernels for 66% -> 67%
where the time goes in v3:
time: 178 us
  Pallas kernels  120 us (67%)
  local copies, waits for them, and re-layouts  21.4 us (12%)
  between operations  14.1 us (8%)
  matrix products  9.9 us (6%)
  starting transfers between devices  6.97 us (4%)
  other arithmetic  3.18 us (2%)
  waiting for transfers between devices  2.44 us (1%)
    pallas_call x1, Pallas kernels, dense_part(): pl.pallas_call(functools.partial(dense_kernel, chips, groups == 2, rows,...  94 us
    pallas_call x1, Pallas kernels, gather_small(): pl.pallas_call(functools.partial(gather_kernel, chips, groups == 2), out_...  26 us
    reshape x2, local copies, waits for them, and re-layouts, shards(): part_up.reshape(devices, -1, rank)  6.48 us
    dot_general x2, matrix products, dot_tn(): lax.dot_general(left, right, (((0,), (0,)), ((), ())), preferred_element_...  5.73 us
    dot_general x1, matrix products, shards(): jnp.dot(output_gradient, up_all, preferred_element_type=jnp.float32)  4.17 us
    transpose x2, local copies, waits for them, and re-layouts, shards(): jnp.transpose(packed[:, :, rows:rows + width], (0, 2, 1)).reshape(-1, rank)  3.83 us
  transfers between devices with their start and end apart: 6, of which 2 were waited for; matrix products, arithmetic and copies ran while one was open for 15% of the time, Pallas kernels for 67%

profile of v3, /device:TPU:0, one launch (start us, length us, event | category | flops | bytes accessed | tf_op | source)
XLA Modules:
  0.0 178.0 jit_solution(4655018438195177847)
XLA Ops:
  7.2 0.0 copy-start
  7.2 0.0 copy-start.1
  7.2 0.0 copy-start.2
  7.2 0.0 reduce-scatter.2.cloned.1.call-start
  7.3 1.4 slice_select_fusion
  8.6 3.1 %collective-permute-start = (bf16[128,2176]{1,0:T(8,128)(2,1)S(1)}, bf16[128,2176]{1,0:T(8,128)(2,1)S(1)}, u32[]{:S(2)}, u32[]{:S(2)}) collective-permute-start(bf16[128,2176]{1,0:T(8,128)(2,1)S(1)} %slice_select_fusion), channel_id=1, source_target_pairs={{0,4},{1,5},{4,8},{5,9},{8,12},{9,13},{12,14},{13,15},{14,10},{15,... | collective-permute-start | bytes 1671176 | tf_op jit(solution)/shard_map/ppermute | solution.py:250
  11.7 1.9 %slice.31 = bf16[128,2304]{1,0:T(8,128)(2,1)} slice(bf16[128,6656]{1,0:T(8,128)(2,1)} %weight_ref.1), slice={[0:128], [2176:4480]} | slice | bytes 1179648 | tf_op jit(solution)/shard_map/slice | solution.py:249
  13.7 0.0 collective-permute-start.2
  13.7 0.0 copy-done.1
  13.7 0.0 copy-done.2
  13.7 26.0 %shard_map.76 = bf16[16,64,640]{2,1,0:T(8,128)(2,1)S(1)} custom-call(bf16[64,640]{1,0:T(8,128)(2,1)S(1)} %fusion.5.mine_ref), custom_call_target="tpu_custom_call" | custom-call | bytes 41943040 | tf_op jit(solution)/shard_map/pallas_call | solution.py:383
  39.8 1.1 slice_bitcast_fusion
  40.9 0.3 copy.14
  41.2 2.8 %copy.12 = bf16[16,416,64]{1,0,2:T(8,128)(2,1)} copy(bf16[16,416,64]{1,2,0:T(8,128)(2,1)} %slice_bitcast_fusion) | data formatting | bytes 1703936 | tf_op jit(solution)/shard_map/transpose | solution.py:413
  43.9 3.1 %reshape.20 = bf16[6656,64]{0,1:T(8,128)(2,1)} reshape(bf16[16,416,64]{1,0,2:T(8,128)(2,1)} %copy.12) | data formatting | bytes 1703936 | tf_op jit(solution)/shard_map/reshape | solution.py:413
  47.0 0.0 copy-done
  47.0 5.3 %fusion = f32[6656,64]{0,1:T(8,128)} fusion(bf16[384,6656]{1,0:T(8,128)(2,1)} %grad_ref.1, bf16[2048,64]{1,0:T(8,128)(2,1)S(1)} %bitcast.32, bf16[384,2048]{1,0:T(8,128)(2,1)S(1)} %copy-done), kind=kOutput, calls=%fused_computation.1 | convolution fusion | flops 428269568 | bytes 8650752 | tf_op jit(solution)/shard_map/dot_general | solution.py:24
  52.3 0.0 collective-permute-done.ahead_one
  52.3 2.4 %collective-permute-start.1 = (bf16[128,2176]{1,0:T(8,128)(2,1)S(1)}, bf16[128,2176]{1,0:T(8,128)(2,1)S(1)}, u32[]{:S(2)}, u32[]{:S(2)}) collective-permute-start(bf16[128,2176]{1,0:T(8,128)(2,1)S(1)} %collective-permute-done.ahead_one), channel_id=1, source_target_pairs={{0,4},{1,5},{4,8},{5,9},{8,12},{9,13},{12,14},{13,15},{14,10},{15,... | collective-permute-start | bytes 1671176 | tf_op jit(solution)/shard_map/ppermute | solution.py:253
  54.7 1.5 collective-permute-start.4
  56.2 0.0 collective-permute-done.2.behind_one
  56.2 0.0 collective-permute-start.3
  56.2 4.2 %fusion.2 = bf16[64,384]{0,1:T(8,128)(2,1)S(1)} fusion(bf16[6656,64]{0,1:T(8,128)(2,1)} %reshape.20, bf16[384,6656]{1,0:T(8,128)(2,1)} %grad_ref.1), kind=kOutput, calls=%fused_computation.6 | convolution fusion | flops 327204864 | bytes 6012928 | tf_op jit(solution)/shard_map/dot_general | solution.py:418
  60.3 3.7 %reshape.23 = f32[16,416,64]{1,0,2:T(8,128)} reshape(f32[6656,64]{0,1:T(8,128)} %fusion) | data formatting | bytes 3407872 | tf_op jit(solution)/shard_map/reshape | solution.py:423
  64.0 2.8 %copy.16 = f32[16,416,64]{1,2,0:T(8,128)S(1)} copy(f32[16,416,64]{1,0,2:T(8,128)} %reshape.23) | data formatting | bytes 3407872 | tf_op jit(solution)/shard_map/reshape | solution.py:423
  66.8 0.4 fusion.1
  67.3 1.8 pad_maximum_fusion
  69.1 0.0 reduce-scatter.2.cloned.1.call-update
  69.1 0.0 collective-permute-done.1.ahead_two
  69.1 0.3 collective-permute-done.4.across_one
  69.4 2.1 %collective-permute-done.3.behind_two = bf16[128,2304]{1,0:T(8,128)(2,1)} collective-permute-done((bf16[128,2304]{1,0:T(8,128)(2,1)}, bf16[128,2304]{1,0:T(8,128)(2,1)}, u32[]{:S(2)}, u32[]{:S(2)}) %collective-permute-start.3) | collective-permute-done | bytes 589856 | tf_op jit(solution)/shard_map/ppermute | solution.py:254
  71.5 94.0 %shard_map.77 = bf16[384,2048]{1,0:T(8,128)(2,1)} custom-call(bf16[384,6656]{1,0:T(8,128)(2,1)} %grad_ref.1, bf16[128,6656]{1,0:T(8,128)(2,1)} %weight_ref.1, bf16[384,64]{1,0:T(8,128)(2,1)S(1)} %bitcast.34, bf16[2048,64]{1,0:T(8,128)(2,1)S(1)} %bitcast.33, bf16[128,2176]{1,0:T(8,128)(2,1)S(1)} %collective-permute-done.ahead_one, ...), custom_call_target="tpu_custom_call" | custom-call | flops 104689827840 | bytes 163577856 | tf_op jit(solution)/shard_map/pallas_call | solution.py:270
  165.5 0.0 reduce-scatter.2.cloned.1.call-done
  165.5 1.4 slice_bitcast_fusion.3
  166.9 1.6 slice_bitcast_fusion.2
  168.4 2.7 %copy.22 = bf16[384,2048]{1,0:T(8,128)(2,1)} copy(bf16[384,2048]{1,0:T(8,128)(2,1)} %shard_map.77) | data formatting | bytes 3145728
  (3 shorter events, 0.1 us)
Async XLA Ops:
  7.2 39.8 %copy-start = (bf16[384,2048]{1,0:T(8,128)(2,1)S(1)}, bf16[384,2048]{1,0:T(8,128)(2,1)}, u32[]{:S(2)}) copy-start(bf16[384,2048]{1,0:T(8,128)(2,1)} %param.5) | copy-start | bytes 4718596
  7.2 6.5 %copy-start.1 = (bf16[64,416]{1,0:T(8,128)(2,1)S(1)}, bf16[64,416]{1,0:T(8,128)(2,1)}, u32[]{:S(2)}) copy-start(bf16[64,416]{1,0:T(8,128)(2,1)} %param.9) | copy-start | bytes 159748
  7.2 6.5 %copy-start.2 = (bf16[128,64]{0,1:T(8,128)(2,1)S(1)}, bf16[128,64]{0,1:T(8,128)(2,1)}, u32[]{:S(2)}) copy-start(bf16[128,64]{0,1:T(8,128)(2,1)} %param.8) | copy-start | bytes 49156
  7.2 158.3 %reduce-scatter.2.cloned.1.call-start = ((), (), s32[]{:S(2)}) async-start(), calls=%async_computation.1 | async-start | bytes 2785280 | tf_op jit(solution)/shard_map/reduce_scatter | solution.py:426
  8.6 43.7 %collective-permute-start = (bf16[128,2176]{1,0:T(8,128)(2,1)S(1)}, bf16[128,2176]{1,0:T(8,128)(2,1)S(1)}, u32[]{:S(2)}, u32[]{:S(2)}) collective-permute-start(bf16[128,2176]{1,0:T(8,128)(2,1)S(1)} %slice_select_fusion), channel_id=1, source_target_pairs={{0,4},{1,5},{4,8},{5,9},{8,12},{9,13},{12,14},{13,15},{14,10},{15,... | collective-permute-start | bytes 1671176 | tf_op jit(solution)/shard_map/ppermute | solution.py:250
  13.7 42.5 %collective-permute-start.2 = (bf16[128,2304]{1,0:T(8,128)(2,1)}, bf16[128,2304]{1,0:T(8,128)(2,1)}, u32[]{:S(2)}, u32[]{:S(2)}) collective-permute-start(bf16[128,2304]{1,0:T(8,128)(2,1)} %slice.31), channel_id=1, source_target_pairs={{4,0},{5,1},{8,4},{9,5},{12,8},{13,9},{14,12},{15,13},{10,14},{11,... | collective-permute-start | bytes 1769480 | tf_op jit(solution)/shard_map/ppermute | solution.py:251
  52.3 16.8 %collective-permute-start.1 = (bf16[128,2176]{1,0:T(8,128)(2,1)S(1)}, bf16[128,2176]{1,0:T(8,128)(2,1)S(1)}, u32[]{:S(2)}, u32[]{:S(2)}) collective-permute-start(bf16[128,2176]{1,0:T(8,128)(2,1)S(1)} %collective-permute-done.ahead_one), channel_id=1, source_target_pairs={{0,4},{1,5},{4,8},{5,9},{8,12},{9,13},{12,14},{13,15},{14,10},{15,... | collective-permute-start | bytes 1671176 | tf_op jit(solution)/shard_map/ppermute | solution.py:253
  54.7 14.7 %collective-permute-start.4 = (bf16[128,2176]{1,0:T(8,128)(2,1)S(1)}, bf16[128,2176]{1,0:T(8,128)(2,1)}, u32[]{:S(2)}, u32[]{:S(2)}) collective-permute-start(bf16[128,2176]{1,0:T(8,128)(2,1)S(1)} %collective-permute-done.ahead_one), channel_id=1, source_target_pairs={{0,16},{16,0},{1,17},{17,1},{2,18},{18,2},{3,19},{19,3},{4,20},{20... | collective-permute-start | bytes 1671176 | tf_op jit(solution)/shard_map/ppermute | solution.py:252
  56.2 15.3 %collective-permute-start.3 = (bf16[128,2304]{1,0:T(8,128)(2,1)}, bf16[128,2304]{1,0:T(8,128)(2,1)}, u32[]{:S(2)}, u32[]{:S(2)}) collective-permute-start(bf16[128,2304]{1,0:T(8,128)(2,1)} %collective-permute-done.2.behind_one), channel_id=1, source_target_pairs={{4,0},{5,1},{8,4},{9,5},{12,8},{13,9},{14,12},{15,13},{10,14},{11,... | collective-permute-start | bytes 1769480 | tf_op jit(solution)/shard_map/ppermute | solution.py:254
Sparse Core Ops, SparseCore 0:
  69.2 78.2 reduce-scatter.1
